TPU v7x, 512 devices: a whole 4x4x16 slice. The times are simulated.
512 devices in a mesh: wide: 64 (over z, y), narrow: 8 (over x, core).
Axes of the slice: x: 4, y: 4, z: 16, core: 2. Of those that a mesh axis runs over, the one named last changes fastest.
Arguments:
- right_side: float32 [512, 32, 1024], P('wide', None, 'narrow'), may hold values from -8 to 8
- conductivity: float32 [512, 32, 1024], P('wide', None, 'narrow'), may hold values from 0.1 to 10
Outputs:
- solution: float32 [512, 32, 1024], P('wide', None, 'narrow')
All inputs are finite; a program needn't handle non-finite values.
Results may differ from a plain program's by a relative error of at most 0.00002.
Values sent between devices are 32-bit elements; how exact they have to be, the bound alone decides.
A program may use at most 128 MiB of HBM per device.

v0:
```python
import functools

import jax
import jax.numpy as jnp
from jax import lax
from jax.experimental import pallas as pl
from jax.experimental.pallas import tpu as pltpu
from jax.sharding import PartitionSpec as P

CENTER = 1.125
HALF = 0.875
LANES = 128
REACH = 8
HALF_REACH = 4
F32 = jnp.float32
MESH_ID = pl.DeviceIdType.MESH


def cheb(sweeps):
    sigma = CENTER / HALF
    steps = [(0.0, 1.0 / CENTER)]
    ratio = 1.0 / sigma
    for _ in range(sweeps - 1):
        ratio_next = 1.0 / (2.0 * sigma - ratio)
        steps.append((ratio_next * ratio, 2.0 * ratio_next / HALF))
        ratio = ratio_next
    return steps


def over_sides(first, second, count, body):
    for base in (first, second):
        for at in range(count):
            body(base + at)


def over_layers(low, high, unroll, body):
    count = high - low + 1
    if count == unroll:
        for at in range(low, high + 1):
            body(at)
        return

    def block(step, carry):
        for at in range(unroll):
            body(low + step * unroll + at)
        return carry

    lax.fori_loop(0, count // unroll, block, 0)


class Level:
    def __init__(self, refs, scale, rows, row_step, lane_step, base, extent, lane_mask):
        self.c, self.s, self.cx, self.cy, self.cz, self.iv, self.dg, self.va, self.vb = refs
        self.half = 0.5 * scale
        self.rows, self.row_step, self.lane_step = rows, row_step, lane_step
        self.base, self.extent, self.lane_mask = base, extent, lane_mask

    def inside(self, at):
        where_x = self.base + at
        return jnp.where((where_x >= 0) & (where_x < self.extent), 1.0, 0.0).astype(F32)

    def lane(self):
        return lax.broadcasted_iota(jnp.int32, (self.rows, LANES), 1)

    def row(self):
        return lax.broadcasted_iota(jnp.int32, (self.rows, LANES), 0)

    def y_up(self, tile):
        return pltpu.roll(tile, self.rows - self.row_step, 0)

    def y_down(self, tile):
        return pltpu.roll(tile, self.row_step, 0)

    def turned(self, tiles, shift, edge, count):
        out = [pltpu.roll(t, shift, 1) for t in tiles]
        if len(tiles) == 1:
            return out
        at_edge = self.lane() == edge
        return [jnp.where(at_edge, out[1 - k], out[k]) for k in range(count)]

    def z_up(self, tiles, count):
        return self.turned(tiles, LANES - self.lane_step, LANES - 1, count)

    def z_down(self, tiles, count):
        return self.turned(tiles, self.lane_step, 0, count)

    def masked(self, at, tiles):
        keep = self.inside(at) * self.half
        out = []
        for k in range(tiles):
            mask = self.lane_mask[k]
            out.append(self.c[k, at] * (keep if mask is None else mask * keep))
        return out

    def setup_below(self, low, tiles):
        first, second = self.masked(low - 1, tiles), self.masked(low, tiles)
        for k in range(tiles):
            self.cx[k, low - 1] = first[k] + second[k]

    def setup_at(self, at, tiles):
        before, here, after = self.masked(at - 1, tiles), self.masked(at, tiles), self.masked(at + 1, tiles)
        inside = self.inside(at)
        top = self.row() >= self.rows - self.row_step
        bottom = self.row() < self.row_step
        z_up, z_down = self.z_up(here, tiles), self.z_down(here, tiles)
        for k in range(tiles):
            own = here[k]
            x_low = before[k] + own
            x_high = own + after[k]
            y_low = own + jnp.where(bottom, 0.0, self.y_down(own))
            y_high = own + jnp.where(top, 0.0, self.y_up(own))
            z_low = own + z_down[k]
            z_high = own + z_up[k]
            diagonal = x_low + x_high + y_low + y_high + z_low + z_high
            keep = inside if self.lane_mask[k] is None else self.lane_mask[k] * inside
            self.cx[k, at] = x_high
            self.cy[k, at] = jnp.where(top, 0.0, y_high)
            self.cz[k, at] = z_high
            if k == 0:
                self.dg[0, at] = diagonal
            self.iv[k, at] = jnp.where(jnp.full_like(own, 0.0) + keep > 0.5, 1.0 / diagonal, 0.0)

    def setup(self, low, high, unroll, tiles):
        self.setup_below(low, tiles)
        over_layers(low, high, unroll, lambda at: self.setup_at(at, tiles))

    def start_at(self, at, tiles, beta):
        for k in range(tiles):
            self.va[k, at] = self.s[k, at] * self.iv[k, at] * beta

    def start_outer(self, at, beta):
        self.va[1, at] = self.s[1, at] * self.iv[1, at] * beta

    def start(self, low, high, unroll, tiles, beta):
        over_layers(low, high, unroll, lambda at: self.start_at(at, tiles, beta))

    def around(self, field, at, tiles, count):
        here = [field[k, at] for k in range(tiles)]
        cz = [self.cz[k, at] for k in range(tiles)]
        z_up = self.z_up(here, count)
        z_down = self.z_down([cz[k] * here[k] for k in range(tiles)], count)
        sums = []
        for k in range(count):
            cy = self.cy[k, at]
            total = self.cx[k, at] * field[k, at + 1] + self.cx[k, at - 1] * field[k, at - 1]
            total = total + (cy * self.y_up(here[k]) + self.y_down(cy * here[k]))
            total = total + (cz[k] * z_up[k] + z_down[k])
            sums.append(total + self.s[k, at])
        return here, sums

    def sweep_at(self, at, field, result, tiles, count, step, fresh):
        alpha, beta = step
        here, sums = self.around(field, at, tiles, count)
        for k in range(count):
            kept = (1.0 + alpha - beta) * here[k]
            if not fresh:
                kept = kept - alpha * result[k, at]
            result[k, at] = kept + (beta * self.iv[k, at]) * sums[k]

    def sweep(self, field, result, low, high, unroll, tiles, count, step, fresh=False):
        over_layers(low, high, unroll, lambda at: self.sweep_at(at, field, result, tiles, count, step, fresh))

    def residual_at(self, at, field, result, tiles):
        here, sums = self.around(field, at, tiles, 1)
        result[0, at] = sums[0] - self.dg[0, at] * here[0]

    def residual(self, field, result, low, high, unroll, tiles):
        over_layers(low, high, unroll, lambda at: self.residual_at(at, field, result, tiles))

    def last_at(self, at, field, older, step):
        alpha, beta = step
        here, sums = self.around(field, at, 1, 1)
        return (1.0 + alpha - beta) * here[0] - alpha * older[0, at], (beta * self.iv[0, at]) * sums[0]


class Strips:
    def __init__(self, refs, base, extent, left, right):
        self.c, self.s, self.cx, self.cy, self.cz, self.iv, self.dg, self.va, self.vb = refs
        self.base, self.extent, self.left, self.right = base, extent, left, right

    def lane(self):
        return lax.broadcasted_iota(jnp.int32, (32, LANES), 1)

    def mask(self, pack):
        where_x = self.base + 4 * pack + self.lane() // 32
        cell = self.lane() % 32
        keep = jnp.where(cell < 8, self.left, jnp.where(cell >= 24, self.right, 1.0))
        return jnp.where((where_x >= 0) & (where_x < self.extent), keep, 0.0)

    def x_up(self, tiles):
        turned = [pltpu.roll(t, LANES - 32, 1) for t in tiles]
        return [jnp.where(self.lane() < LANES - 32, turned[p], turned[min(p + 1, 3)]) for p in range(4)]

    def x_down(self, tiles):
        turned = [pltpu.roll(t, 32, 1) for t in tiles]
        return [jnp.where(self.lane() >= 32, turned[p], turned[max(p - 1, 0)]) for p in range(4)]

    def setup(self):
        row = lax.broadcasted_iota(jnp.int32, (32, LANES), 0)
        top, bottom = row == 31, row == 0
        masks = [self.mask(p) for p in range(4)]
        own = [self.c[p] * (0.5 * masks[p]) for p in range(4)]
        above = self.x_up(own)
        x_high = [own[p] + above[p] for p in range(4)]
        x_low = self.x_down(x_high)
        for p in range(4):
            y_high = own[p] + jnp.where(top, 0.0, pltpu.roll(own[p], 31, 0))
            y_low = jnp.where(bottom, own[p], pltpu.roll(y_high, 1, 0))
            z_high = own[p] + pltpu.roll(own[p], LANES - 1, 1)
            z_low = pltpu.roll(z_high, 1, 1)
            diagonal = x_low[p] + x_high[p] + y_low + y_high + z_low + z_high
            self.cx[p] = x_high[p]
            self.cy[p] = jnp.where(top, 0.0, y_high)
            self.cz[p] = z_high
            self.dg[p] = diagonal
            self.iv[p] = jnp.where(masks[p] > 0.5, 1.0 / diagonal, 0.0)

    def start(self, beta):
        for p in range(4):
            self.va[p] = self.s[p] * self.iv[p] * beta

    def around(self, field):
        here = [field[p] for p in range(4)]
        cx = [self.cx[p] for p in range(4)]
        x_up = self.x_up(here)
        x_down = self.x_down([cx[p] * here[p] for p in range(4)])
        sums = []
        for p in range(4):
            cy, cz = self.cy[p], self.cz[p]
            total = cx[p] * x_up[p] + x_down[p]
            total = total + (cy * pltpu.roll(here[p], 31, 0) + pltpu.roll(cy * here[p], 1, 0))
            total = total + (cz * pltpu.roll(here[p], LANES - 1, 1) + pltpu.roll(cz * here[p], 1, 1))
            sums.append(total + self.s[p])
        return here, sums

    def sweep(self, field, result, step, fresh=False):
        alpha, beta = step
        here, sums = self.around(field)
        for p in range(4):
            kept = (1.0 + alpha - beta) * here[p]
            if not fresh:
                kept = kept - alpha * result[p]
            result[p] = kept + (beta * self.iv[p]) * sums[p]

    def residual(self, field, result):
        here, sums = self.around(field)
        for p in range(4):
            result[p] = sums[p] - self.dg[p] * here[p]

    def own(self, ref, pack, layers=range(4)):
        cell = self.lane() % 32
        packed = jnp.zeros((32, LANES), F32)
        for layer in layers:
            tile = ref[0, 4 * pack + layer]
            first = pltpu.roll(tile, 32 * layer + 8, 1)
            last = pltpu.roll(tile, (32 * layer + 24) % LANES, 1)
            packed = jnp.where(self.lane() // 32 == layer, jnp.where(cell < 16, first, last), packed)
        return packed

    def take_halo(self, ref, pack, from_left, from_right):
        cell = lax.broadcasted_iota(jnp.int32, (8, LANES), 1) % 32
        for part in range(4):
            rows = pl.ds(8 * part, 8)
            below = pltpu.roll(from_left, (LANES - 8 * part) % LANES, 1)
            above = pltpu.roll(from_right, 24 - 8 * part, 1) if part < 3 else from_right
            ref[pack, rows, :] = jnp.where(cell < 8, below, jnp.where(cell >= 24, above, ref[pack, rows, :]))

    def give_halo(self, ref, pack, side):
        cell = lax.broadcasted_iota(jnp.int32, (8, LANES), 1) % 32
        packed = None
        for part in range(4):
            shift = (8 * part - 8 - 8 * side) % LANES
            tile = ref[pack, pl.ds(8 * part, 8), :]
            tile = pltpu.roll(tile, shift, 1) if shift else tile
            packed = tile if part == 0 else jnp.where(cell // 8 == part, tile, packed)
        return packed

    def mend(self, tile, ref, at):
        packed, layer = ref[at // 4], at % 4
        first = pltpu.roll(packed, (LANES - 32 * layer - 8) % LANES, 1)
        last = pltpu.roll(packed, (LANES + 104 - 32 * layer) % LANES, 1)
        return jnp.where(self.lane() < 4, first, jnp.where(self.lane() >= LANES - 4, last, tile))


LEVEL_FIELDS = 9
LEVEL_SHAPES = ((1, 16, 32, LANES), (2, 14, 16, LANES), (1, 34, 8, LANES), (1, 15, 8, LANES))
RULER = 1024
SENDERS = 10 + 2 * (2 * REACH + 1)
GROUPS = 34 + 2 * (2 * REACH + 1)


def kernel(wide, narrow, rhs, coef, kept, added, *scratch):
    scratch = list(scratch)
    level_refs = []
    for _ in range(4):
        level_refs.append(scratch[:LEVEL_FIELDS])
        scratch = scratch[LEVEL_FIELDS:]
    strip_refs, scratch = scratch[:LEVEL_FIELDS], scratch[LEVEL_FIELDS:]
    (ps, zs, rz, rcn, kp, k1cx, k1c, sk, sp, k1x, k1p, k1z, rc2, s2m, rs2, rx1, sb0, hx0, p1, p0, ruler,
     local_sem, send_sem, recv_sem) = scratch
    me_w = lax.axis_index("wide")
    me_n = lax.axis_index("narrow")

    def there(dw, dn):
        return (lax.rem(me_w + (dw + wide), wide), lax.rem(me_n + (dn + narrow), narrow))

    has = (me_w > 0, me_w < wide - 1)
    has_z = (me_n > 0, me_n < narrow - 1)
    reach = (jnp.minimum(me_w, REACH), jnp.minimum(wide - 1 - me_w, REACH))

    def for_far(first, body, last=REACH):
        for side in range(2):
            sign = 2 * side - 1

            def step(k, carry):
                body(REACH + sign * k, sign * k)
                return carry

            lax.fori_loop(first, jnp.minimum(reach[side], last) + 1, step, 0)

    def for_all_far(body):
        inner = reach[0] + reach[1] == 2 * REACH

        @pl.when(inner)
        def straight():
            for k in range(REACH, 0, -1):
                for sign in (-1, 1):
                    body(REACH + sign * k, sign * k)

        pl.when(jnp.logical_not(inner))(functools.partial(for_far, 1, body))

    def for_sides(body):
        for side in range(2):
            pl.when(has[side])(functools.partial(body, side, 2 * side - 1))

    def for_sides_z(body):
        for side in range(2):
            pl.when(has_z[side])(functools.partial(body, side, 2 * side - 1))

    def for_corners(body):
        for side in range(2):
            for side_z in range(2):
                pl.when(has[side] & has_z[side_z])(
                    functools.partial(body, side, side_z, 2 * side - 1, 2 * side_z - 1)
                )

    @pl.when((me_n == 0) | (me_n == narrow - 1))
    def clear_z():
        for ref in (rz, rcn, k1c, k1z, k1p):
            ref[...] = jnp.zeros(ref.shape, F32)

    @pl.when((me_w < REACH) | (me_w >= wide - REACH))
    def clear():
        def zero(ref):
            ref[...] = jnp.zeros(ref.shape, F32)

        for ref in (rcn, rx1, hx0, rc2, rs2, k1cx, k1c, k1x, k1p):
            zero(ref)
        for side in range(2):
            for ref in level_refs[0][:2]:
                zero(ref.at[0, pl.ds(12 * side, 4)])
            zero(level_refs[1][0].at[0, 13 * side])

    def if_reach(least, body):
        for side in range(2):
            pl.when(reach[side] >= least)(functools.partial(body, side, 2 * side - 1))

    barrier = pltpu.get_barrier_semaphore()

    def greet(dw, dn):
        pl.semaphore_signal(barrier, inc=1, device_id=there(dw, dn), device_id_type=MESH_ID)

    for_far(1, lambda slot, dw: greet(dw, 0), HALF_REACH)
    for_sides_z(lambda side, dn: greet(0, dn))
    for_corners(lambda side, side_z, dw, dn: greet(dw, dn))

    c0, s0 = level_refs[0][0], level_refs[0][1]
    load_c = pltpu.make_async_copy(coef, c0.at[0, pl.ds(4, 8)], local_sem.at[0])
    load_s = pltpu.make_async_copy(rhs, s0.at[0, pl.ds(4, 8)], local_sem.at[1])
    load_c.start()
    load_s.start()
    beside_x = jnp.where(has[0], 1, 0) + jnp.where(has[1], 1, 0)
    beside_z = jnp.where(has_z[0], 1, 0) + jnp.where(has_z[1], 1, 0)
    greeted = beside_z + beside_x * beside_z
    for side in range(2):
        greeted = greeted + jnp.minimum(reach[side], HALF_REACH)

    left = jnp.where(me_n > 0, 1.0, 0.0).astype(F32)
    right = jnp.where(me_n < narrow - 1, 1.0, 0.0).astype(F32)

    def lanes(rows):
        return lax.broadcasted_iota(jnp.int32, (rows, LANES), 1)

    def edges(rows, until, low, since, high):
        at = lanes(rows)
        return jnp.where(at < until, low, jnp.where(at >= since, high, 0.0))

    def centred(rows):
        at = lanes(rows)
        return jnp.where((at >= 32) & (at < 96), 1.0, edges(rows, 32, left, 96, right))

    level_0 = Level(level_refs[0], 1.0, 32, 1, 1, 8 * me_w - 4, 8 * wide, [None])
    strips = Strips(strip_refs, 8 * me_w - 4, 8 * wide, left, right)
    level_1 = Level(
        level_refs[1], 0.25, 16, 1, 1, 4 * me_w - 5, 4 * wide, [centred(16), edges(16, 32, right, 96, left)]
    )
    level_2 = Level(level_refs[2], 0.0625, 8, 1, 2, 2 * me_w - 16, 2 * wide, [centred(8)])
    level_3 = Level(level_refs[3], 0.015625, 8, 2, 4, me_w - 7, wide, [centred(8)])

    sent = [0] * SENDERS

    def send(group, src, dst, dw, dn, rows, sender):
        if isinstance(sender, int):
            sent[sender] += rows
        pltpu.make_async_remote_copy(
            src_ref=src, dst_ref=dst, send_sem=send_sem.at[sender], recv_sem=recv_sem.at[group],
            device_id=there(dw, dn), device_id_type=MESH_ID,
        ).start()

    def ruled(rows, group, sender):
        span = ruler.at[pl.ds(0, rows)]
        return pltpu.make_async_remote_copy(
            src_ref=span, dst_ref=span, send_sem=send_sem.at[sender], recv_sem=recv_sem.at[group],
            device_id=there(0, 1), device_id_type=MESH_ID,
        )

    def receive(group, rows):
        ruled(rows, group, 0).wait_recv()

    def receive_sides(group, rows):
        for_sides(lambda side, dw: receive(group + side, rows))

    def receive_sides_z(group, rows):
        for_sides_z(lambda side, dn: receive(group + side, rows))

    def receive_corners(group, rows):
        for_corners(lambda side, side_z, dw, dn: receive(group + 2 * side + side_z, rows))

    def receive_far(group, last=REACH):
        for_far(1, lambda slot, dw: receive(group + slot, 8), last)

    def sends_done(sender):
        ruled(sent[sender], 0, sender).wait_send()

    from_z, from_s1z = 0, 2
    from_c_corner, from_k_corner, from_s1_corner = 4, 8, 12
    from_c, from_s, from_s_next, from_k, from_s1, from_c1b, from_x0, from_x1 = range(16, 32, 2)
    from_four = 32
    from_c2 = 34
    from_s2 = from_c2 + 2 * REACH + 1
    sender_x, sender_four, sender_z = range(0, 6, 2)
    sender_corner, sender_c2, sender_far = 6, 10, 10 + 2 * REACH + 1

    def restrict_0(ref):
        out = []
        for layer in range(4):
            total = None
            for dx in range(2):
                for dy in range(2):
                    term = ref[0, 4 + 2 * layer + dx, pl.ds(dy, 16, stride=2), :]
                    total = term if total is None else total + term
            total = total + pltpu.roll(total, LANES - 1, 1)
            out.append(0.125 * jnp.take_along_axis(total, (2 * lanes(16) + 64) % LANES, axis=1))
        return out

    odd_8 = lanes(8) % 2 == 1

    def pairs_1(ref):
        out = []
        for layer in range(2):
            total = None
            for dx in range(2):
                for dy in range(2):
                    term = ref[0, 5 + 2 * layer + dx, pl.ds(dy, 8, stride=2), :]
                    total = term if total is None else total + term
            total = total + jnp.where(odd_8, pltpu.roll(total, 1, 1), pltpu.roll(total, LANES - 1, 1))
            out.append(0.125 * total)
        return jnp.where(odd_8, out[1], out[0])

    def squeeze_1(layers, ref, row):
        for part in range(2):
            ref[pl.ds(row + 16 * part, 16), :] = jnp.where(lanes(16) < 64, layers[part], layers[part + 2])

    def squeeze_halves(first, second):
        low_quarter = lanes(16) % 64 < 32
        return (
            jnp.where(low_quarter, pltpu.roll(first, 96, 1), second),
            jnp.where(low_quarter, first, pltpu.roll(second, 32, 1)),
        )

    load_c.wait()
    own_c1 = restrict_0(c0)
    for half in range(2):
        strips.c[1 + half] = strips.own(c0, 1 + half)
    for side in range(2):
        squeeze_1(own_c1, zs.at[side], 32)
        for half in range(2):
            zs[side, pl.ds(16 * half, 8), :] = strips.give_halo(strips.c, 1 + half, side)
    load_s.wait()
    for half in range(2):
        strips.s[1 + half] = strips.own(s0, 1 + half)
    for side in range(2):
        for half in range(2):
            zs[side, pl.ds(16 * half + 8, 8), :] = strips.give_halo(strips.s, 1 + half, side)

    pl.semaphore_wait(barrier, greeted)

    @for_sides
    def send_faces(side, dw):
        src, dst = c0.at[0, pl.ds(4 + 4 * side, 4)], c0.at[0, pl.ds(12 - 12 * side, 4)]
        send(from_c + 1 - side, src, dst, dw, 0, 128, sender_x + side)

    @for_sides
    def send_nearest(side, dw):
        send(from_s + 1 - side, s0.at[0, 4 + 7 * side], s0.at[0, 12 - 9 * side], dw, 0, 32, sender_x + side)

    for_sides_z(
        lambda side, dn: send(from_z + 1 - side, zs.at[side], rz.at[1 - side], 0, dn, 64, sender_z + side)
    )

    def send_corner(group, src, dst, rows, side, side_z):
        at = 2 * side + side_z
        send(group + 3 - at, src, dst, 2 * side - 1, 2 * side_z - 1, rows, sender_corner + at)

    @for_corners
    def send_c_corner(side, side_z, dw, dn):
        src = zs.at[side_z, pl.ds(16 * side, 16)]
        send_corner(from_c_corner, src, rcn.at[1 - side, 1 - side_z], 16, side, side_z)

    @for_sides
    def send_s_next(side, dw):
        src = s0.at[0, pl.ds(5 + 4 * side, 2)]
        send(from_s_next + 1 - side, src, s0.at[0, pl.ds(13 - 12 * side, 2)], dw, 0, 64, sender_x + side)

    steps = cheb(3)
    sweep_a = (level_0.va, level_0.vb, 1, 1, steps[1], True)
    sweep_b = (level_0.vb, level_0.va, 1, 1, steps[2], False)
    level_0.setup(5, 10, 6, 1)
    level_0.start(5, 10, 6, 1, steps[0][1])
    over_layers(6, 9, 4, lambda at: level_0.sweep_at(at, *sweep_a))
    over_layers(7, 8, 2, lambda at: level_0.sweep_at(at, *sweep_b))

    def take_halos(field, ref, pack, got):
        rows = pl.ds(8 * field + (16 if pack == 2 else 0), 8)
        strips.take_halo(ref, pack, got[0, rows, :], got[1, rows, :])

    receive_sides_z(from_z, 64)
    for field, ref in enumerate((strips.c, strips.s)):
        for half in range(2):
            take_halos(field, ref, 1 + half, rz)

    def spread_1(ref, block):
        at_lane = lanes(16)
        low_half = at_lane < 64
        low_quarter = at_lane % 64 < 32
        for part in range(2):
            before, own, after = (block(dz, part) for dz in (-1, 0, 1))
            near = jnp.where(low_quarter, before, after)
            outer = jnp.where(low_quarter, after, before)
            own_r, near_r, outer_r = (pltpu.roll(t, 64, 1) for t in (own, near, outer))
            at = 5 + part
            for at, own_a, own_b, near_a, near_b, outer_a, outer_b in (
                (at, own, own_r, near, near_r, outer, outer_r),
                (at + 2, own_r, own, near_r, near, outer_r, outer),
            ):
                centre = jnp.where(low_half, own_a, own_b)
                ref[0, at] = jnp.where(at_lane < 32, near_a, jnp.where(at_lane < 96, centre, near_b))
                ref[1, at] = jnp.where(low_half, outer_a, outer_b)

    def coef_block(dz, part):
        rows = pl.ds(32 + 16 * part, 16)
        return zs[0, rows, :] if dz == 0 else rz[(1 + dz) // 2, rows, :]

    spread_1(level_1.c, coef_block)
    rc2[REACH] = pairs_1(level_1.c)

    for_far(
        1,
        lambda slot, dw: send(
            from_c2 + 2 * REACH - slot, rc2.at[REACH], rc2.at[2 * REACH - slot], dw, 0, 8, sender_c2 + slot
        ),
        HALF_REACH,
    )
    k1_own = zs.at[0, pl.ds(32, 32)]
    halves = squeeze_halves(zs[0, pl.ds(32, 16), :], zs[0, pl.ds(48, 16), :])
    at_lane = lanes(16)
    for side in range(2):
        near, far = (0, 3) if side == 0 else (3, 0)
        full = level_1.c[0, 5 + near]
        place = (32 * far + 31, 32 * far)
        cell = (64, 63)
        for side_z in range(2):
            moved = pltpu.roll(full, (place[side_z] - cell[side_z]) % LANES, 1)
            kp[side, side_z] = jnp.where(at_lane == place[side_z], moved, halves[side_z])
    for_sides(
        lambda side, dw: send(from_k + 1 - side, k1_own, k1cx.at[1 - side], dw, 0, 32, sender_x + side)
    )
    for_corners(
        lambda side, side_z, dw, dn: send_corner(
            from_k_corner, kp.at[side, side_z], k1c.at[1 - side, 1 - side_z], 16, side, side_z
        )
    )

    receive_sides(from_c, 128)
    receive_corners(from_c_corner, 16)
    for side in range(2):
        strips.c[3 * side] = strips.own(c0, 3 * side)
        take_halos(0, strips.c, 3 * side, rcn.at[side])
    level_0.setup_below(1, 1)
    over_sides(1, 11, 4, lambda at: level_0.setup_at(at, 1))
    strips.setup()
    receive_sides(from_s, 32)
    over_sides(3, 11, 2, lambda at: level_0.start_at(at, 1, steps[0][1]))
    over_sides(4, 10, 2, lambda at: level_0.sweep_at(at, *sweep_a))
    over_sides(5, 9, 2, lambda at: level_0.sweep_at(at, *sweep_b))
    over_layers(6, 9, 4, lambda at: level_0.residual_at(at, level_0.va, level_0.vb, 1))
    receive_sides(from_s_next, 64)
    for side in range(2):
        strips.s[3 * side] = strips.own(s0, 3 * side, range(1 - side, 4 - side))
        take_halos(1, strips.s, 3 * side, rcn.at[side])
    over_sides(1, 13, 2, lambda at: level_0.start_at(at, 1, steps[0][1]))
    strips.start(steps[0][1])
    over_sides(2, 12, 2, lambda at: level_0.sweep_at(at, *sweep_a))
    strips.sweep(strips.va, strips.vb, steps[1], fresh=True)
    over_sides(3, 11, 2, lambda at: level_0.sweep_at(at, *sweep_b))
    strips.sweep(strips.vb, strips.va, steps[2])
    over_sides(4, 10, 2, lambda at: level_0.residual_at(at, level_0.va, level_0.vb, 1))
    strips.residual(strips.va, strips.vb)
    for at in range(4, 12):
        level_0.vb[0, at] = strips.mend(level_0.vb[0, at], strips.vb, at)

    squeeze_1(restrict_0(level_0.vb), sk, 0)

    sp[0], sp[1] = squeeze_halves(sk[pl.ds(0, 16), :], sk[pl.ds(16, 16), :])

    for_sides(lambda side, dw: send(from_s1 + 1 - side, sk, k1x.at[1 - side], dw, 0, 32, sender_x + side))
    for_corners(
        lambda side, side_z, dw, dn: send_corner(
            from_s1_corner, sp.at[side_z], k1p.at[1 - side, 1 - side_z], 16, side, side_z
        )
    )
    for_sides_z(lambda side, dn: send(from_s1z + 1 - side, sk, k1z.at[1 - side], 0, dn, 32, sender_z + side))

    receive_far(from_c2, HALF_REACH)

    @functools.partial(if_reach, HALF_REACH)
    def send_four(side, sign):
        src, dst = rc2.at[pl.ds(9 - 5 * side, 4)], rc2.at[pl.ds(13 - 13 * side, 4)]
        send(from_four + 1 - side, src, dst, HALF_REACH * sign, 0, 32, sender_four + side)

    for at in range(3, 13):
        level_0.va[0, at] = strips.mend(level_0.va[0, at], strips.va, at)
    own_cell = (strips.lane() % 32 >= 8) & (strips.lane() % 32 < 24)
    for pack_at, layers in enumerate(((3,), range(4), range(4), (0,))):
        strips.va[pack_at] = jnp.where(own_cell, strips.own(level_0.va, pack_at, layers), strips.va[pack_at])
    for side in range(2):
        first = 9 if side == 0 else 5
        for layer in range(2):
            sb0[side, pl.ds(32 * layer, 32), :] = level_0.va[0, first + layer]
        packed = strips.va[2 - side]
        middle = (lanes(16) >= 32) & (lanes(16) < 96)
        sb0[side, pl.ds(64, 16), :] = jnp.where(middle, packed[:16], pltpu.roll(packed[16:], 64, 1))

    @for_sides
    def send_iterate_0(side, dw):
        send(from_x0 + 1 - side, sb0.at[1 - side], hx0.at[1 - side], dw, 0, 80, sender_x + side)

    def source_block(dz, part):
        rows = pl.ds(16 * part, 16)
        return sk[rows, :] if dz == 0 else k1z[(1 + dz) // 2, rows, :]

    def spread_beside(ref, blocks, packs):
        at_lane = lanes(16)
        low_half = at_lane < 64
        for side in range(2):
            for layer in range(4):
                own = blocks[side, pl.ds(16 * (layer % 2), 16), :]
                other = pltpu.roll(own, 64, 1)
                centre = jnp.where(low_half, own, other) if layer < 2 else jnp.where(low_half, other, own)
                before = pltpu.roll(packs[side, 0], (LANES - 32 * layer) % LANES, 1)
                after = pltpu.roll(packs[side, 1], (LANES + 96 - 32 * layer) % LANES, 1)
                ref[0, 1 + 8 * side + layer] = jnp.where(at_lane < 32, before, jnp.where(at_lane < 96, centre, after))

    receive_sides(from_k, 32)
    receive_corners(from_k_corner, 16)
    spread_beside(level_1.c, k1cx, k1c)
    for side in range(2):
        far = 3 if side == 1 else 0
        below, above = (pltpu.roll(k1c[side, side_z], (shift - 32 * far) % LANES, 1)
                        for side_z, shift in ((0, 127), (1, -31)))
        level_1.c[1, 4 + 5 * side] = jnp.where(lanes(16) < 64, above, below)

    @for_sides
    def send_coef_1(side, dw):
        send(from_c1b + 1 - side, level_1.c.at[0, 9 - 5 * side], level_1.c.at[0, 13 - 13 * side], dw, 0, 16, sender_x + side)

    level_1.setup_below(2, 1)
    over_sides(2, 10, 2, lambda at: level_1.setup_at(at, 1))
    over_layers(4, 9, 6, lambda at: level_1.setup_at(at, 2))

    receive_sides_z(from_s1z, 32)
    spread_1(level_1.s, source_block)
    receive_sides(from_s1, 32)
    receive_corners(from_s1_corner, 16)
    spread_beside(level_1.s, k1x, k1p)
    level_1.start(2, 11, 10, 1, steps[0][1])
    over_layers(5, 8, 4, lambda at: level_1.start_outer(at, steps[0][1]))
    over_sides(3, 9, 2, lambda at: level_1.sweep_at(at, level_1.va, level_1.vb, 1, 1, steps[1], True))
    over_layers(5, 8, 4, lambda at: level_1.sweep_at(at, level_1.va, level_1.vb, 2, 1, steps[1], True))
    level_1.sweep(level_1.vb, level_1.va, 4, 9, 6, 1, 1, steps[2])
    level_1.residual(level_1.va, level_1.vb, 5, 8, 4, 1)

    value = pairs_1(level_1.vb)
    s2m[...] = value
    rs2[REACH] = value

    for_all_far(
        lambda slot, dw: send(
            from_s2 + 2 * REACH - slot, s2m, rs2.at[2 * REACH - slot], dw, 0, 8, sender_far + slot
        )
    )

    @for_sides
    def send_iterate_1(side, dw):
        layers = level_1.va.at[0, pl.ds(6 - 2 * side, 4)]
        send(from_x1 + 1 - side, layers, rx1.at[1 - side], dw, 0, 64, sender_x + side)

    receive_sides(from_c1b, 16)
    level_1.setup_below(1, 1)
    over_sides(1, 12, 1, lambda at: level_1.setup_at(at, 1))

    def spread_2(ref, blocks):
        for block in range(2 * REACH + 1):
            packed = blocks[block]
            ref[0, 2 * block] = jnp.where(odd_8, pltpu.roll(packed, 1, 1), packed)
            ref[0, 2 * block + 1] = jnp.where(odd_8, packed, pltpu.roll(packed, LANES - 1, 1))

    def restrict_2(ref, at):
        total = ref[0, 2 * at + 2] + ref[0, 2 * at + 3]
        odd_row = lax.broadcasted_iota(jnp.int32, (8, LANES), 0) % 2 == 1
        total = total + jnp.where(odd_row, pltpu.roll(total, 1, 0), pltpu.roll(total, 7, 0))
        second = lanes(8) % 4 >= 2
        total = total + jnp.where(second, pltpu.roll(total, 2, 1), pltpu.roll(total, LANES - 2, 1))
        return 0.125 * total

    if_reach(HALF_REACH, lambda side, sign: receive(from_four + side, 32))
    spread_2(level_2.c, rc2)
    level_2.setup(1, 32, 16, 1)
    for at in range(15):
        level_3.c[0, at] = restrict_2(level_2.c, at)
    level_3.setup(1, 13, 13, 1)

    for_sides(lambda side, dw: sends_done(sender_x + side))
    for_sides_z(lambda side, dn: sends_done(sender_z + side))
    for_corners(lambda side, side_z, dw, dn: sends_done(sender_corner + 2 * side + side_z))
    if_reach(HALF_REACH, lambda side, sign: sends_done(sender_four + side))
    for_far(1, lambda slot, dw: ruled(8, 0, sender_c2 + slot).wait_send(), HALF_REACH)
    for_all_far(lambda slot, dw: ruled(8, 0, sender_far + slot).wait_send())

    for_all_far(lambda slot, dw: receive(from_s2 + slot, 8))
    spread_2(level_2.s, rs2)
    level_2.start(1, 32, 32, 1, steps[0][1])
    level_2.sweep(level_2.va, level_2.vb, 2, 31, 30, 1, 1, steps[1], fresh=True)
    level_2.sweep(level_2.vb, level_2.va, 3, 30, 28, 1, 1, steps[2])
    level_2.residual(level_2.va, level_2.vb, 4, 29, 26, 1)

    for at in range(1, 14):
        level_3.s[0, at] = restrict_2(level_2.vb, at)
    coarse = cheb(4)
    level_3.start(1, 13, 13, 1, coarse[0][1])
    level_3.sweep(level_3.va, level_3.vb, 2, 12, 11, 1, 1, coarse[1], fresh=True)
    level_3.sweep(level_3.vb, level_3.va, 3, 11, 9, 1, 1, coarse[2])
    level_3.sweep(level_3.va, level_3.vb, 4, 10, 7, 1, 1, coarse[3])

    for at in range(10, 24):
        level_2.vb[0, at] = level_2.va[0, at] + level_3.vb[0, (at - 2) // 2]
    level_2.sweep(level_2.vb, level_2.va, 11, 22, 12, 1, 1, steps[0], fresh=True)
    level_2.sweep(level_2.va, level_2.vb, 12, 21, 10, 1, 1, steps[1])
    level_2.sweep(level_2.vb, level_2.va, 13, 20, 8, 1, 1, steps[2])

    for at in range(8):
        value = level_2.va[0, 13 + at]
        for part in range(2):
            p1[at, pl.ds(part, 8, stride=2), :] = value
    receive_sides(from_x1, 64)
    for at in range(14):
        if 4 <= at <= 9:
            before = level_1.va[0, at]
        else:
            before = rx1[0, at] if at < 4 else rx1[1, at - 10]
        level_1.vb[0, at] = before + p1[(at + 1) // 2]
    level_1.sweep(level_1.vb, level_1.va, 1, 12, 12, 1, 1, steps[0], fresh=True)
    level_1.sweep(level_1.va, level_1.vb, 2, 11, 10, 1, 1, steps[1])
    level_1.sweep(level_1.vb, level_1.va, 3, 10, 8, 1, 1, steps[2])

    cell = lanes(16) % 32
    strip_lane = jnp.where(cell < 16, 28, 84) + cell // 2
    low_half = lanes(16) < 64
    fine = []
    for at in range(8):
        value = level_1.va[0, 3 + at]
        own = jnp.take_along_axis(value, lanes(16) // 2 + 32, axis=1)
        fine.append(jnp.take_along_axis(value, strip_lane, axis=1))
        for part in range(2):
            p0[at, pl.ds(part, 16, stride=2), :] = own
    for pack in range(4):
        value = jnp.where(low_half, fine[2 * pack], fine[2 * pack + 1])
        for part in range(2):
            ps[pack, pl.ds(part, 16, stride=2), :] = value
    receive_sides(from_x0, 80)
    for side in range(2):
        for layer in range(2):
            at = (1 if side == 0 else 13) + layer
            level_0.vb[0, at] = hx0[side, pl.ds(32 * layer, 32), :] + p0[at // 2]
        packed = hx0[side, pl.ds(64, 16), :]
        layer = lanes(16) // 32
        for part, value in enumerate((packed, pltpu.roll(packed, 64, 1))):
            rows = pl.ds(16 * part, 16)
            own = jnp.where(layer == (3 if side == 0 else 0), strips.va[3 * side, rows, :], 0.0)
            value = jnp.where((layer == 1) | (layer == 2), value, own)
            strips.vb[3 * side, rows, :] = value + ps[3 * side, rows, :]
    for pack in (1, 2):
        strips.vb[pack] = strips.va[pack] + ps[pack]

    def correct(at):
        level_0.vb[0, at] = level_0.va[0, at] + p0[at // 2]

    over_layers(3, 12, 10, correct)
    level_0.sweep(level_0.vb, level_0.va, 2, 13, 12, 1, 1, steps[0], fresh=True)
    strips.sweep(strips.vb, strips.va, steps[0], fresh=True)
    level_0.sweep(level_0.va, level_0.vb, 3, 12, 10, 1, 1, steps[1])
    strips.sweep(strips.va, strips.vb, steps[1])
    strips.sweep(strips.vb, strips.va, steps[2])
    inner = (strips.lane() >= 4) & (strips.lane() < LANES - 4)
    for at in range(4, 12):
        kept_here, added_here = level_0.last_at(at, level_0.vb, level_0.va, steps[2])
        kept[at - 4] = strips.mend(kept_here, strips.va, at)
        added[at - 4] = jnp.where(inner, added_here, 0.0)


def per_device(right_side, conductivity, wide, narrow):
    brick = (8, 32, LANES)
    scratch = []
    for shape in LEVEL_SHAPES:
        scratch += [pltpu.VMEM(shape, F32)] * LEVEL_FIELDS
    scratch += [pltpu.VMEM((4, 32, LANES), F32)] * LEVEL_FIELDS
    shapes = [
        (4, 32, LANES),
        (2, 64, LANES), (2, 64, LANES), (2, 2, 16, LANES),
        (2, 2, 16, LANES), (2, 32, LANES), (2, 2, 16, LANES),
        (32, LANES), (2, 16, LANES), (2, 32, LANES), (2, 2, 16, LANES), (2, 32, LANES),
        (2 * REACH + 1, 8, LANES), (8, LANES), (2 * REACH + 1, 8, LANES),
        (2, 4, 16, LANES),
        (2, 80, LANES), (2, 80, LANES),
        (8, 16, LANES), (8, 32, LANES),
        (RULER, LANES),
    ]
    scratch += [pltpu.VMEM(shape, F32) for shape in shapes]
    scratch += [pltpu.SemaphoreType.DMA((2,)), pltpu.SemaphoreType.DMA((SENDERS,)), pltpu.SemaphoreType.DMA((GROUPS,))]
    kept, added = pl.pallas_call(
        functools.partial(kernel, wide, narrow),
        out_shape=[jax.ShapeDtypeStruct(brick, F32)] * 2,
        in_specs=[pl.BlockSpec(memory_space=pltpu.HBM)] * 2,
        out_specs=[pl.BlockSpec(memory_space=pltpu.VMEM)] * 2,
        scratch_shapes=scratch,
        compiler_params=pltpu.CompilerParams(
            collective_id=0, has_side_effects=True, vmem_limit_bytes=32 * 1024 * 1024
        ),
    )(pltpu.with_memory_space_constraint(right_side, pltpu.HBM), pltpu.with_memory_space_constraint(conductivity, pltpu.HBM))
    return kept + added


def solution(mesh):
    spec = P("wide", None, "narrow")
    body = functools.partial(per_device, wide=mesh.shape["wide"], narrow=mesh.shape["narrow"])
    return jax.shard_map(body, mesh=mesh, in_specs=(spec, spec), out_specs=spec, check_vma=False)
```

profile of v0, /device:TPU:65, one launch (start us, length us, event | category | flops | bytes accessed | tf_op | source)
XLA Modules:
  0.0 27.2 jit_solution(6126510562275068422)
XLA Ops:
  0.0 26.5 %shard_map.28 = (f32[8,32,128]{2,1,0:T(8,128)S(1)}, f32[8,32,128]{2,1,0:T(8,128)S(1)}) custom-call(f32[8,32,128]{2,1,0:T(8,128)} %rhs.1, f32[8,32,128]{2,1,0:T(8,128)} %coef.1), custom_call_target="tpu_custom_call" | custom-call | tf_op jit(solution)/shard_map/pallas_call | solution.py:860
  26.5 0.7 %add.3 = f32[8,32,128]{2,1,0:T(8,128)} add(f32[8,32,128]{2,1,0:T(8,128)S(1)} %get-tuple-element.7, f32[8,32,128]{2,1,0:T(8,128)S(1)} %get-tuple-element.8) | non-fusion elementwise | flops 32768 | bytes 393216 | tf_op jit(solution)/shard_map/add | solution.py:870
where the time goes:
time: 27.3 us; the launch traced here: 27.2 us
  Pallas kernels  26.5 us (97%)
  other arithmetic  0.67 us (2%)
    pallas_call x1, Pallas kernels, per_device(): pl.pallas_call(functools.partial(kernel, wide, narrow), out_shape=[jax.Sh...  26.5 us
    add x1, other arithmetic, per_device(): return kept + added  0.67 us

commit v1 on v0

--- a/solution.py
+++ b/solution.py
@@ -507,8 +507,10 @@
 
     @for_sides
     def send_faces(side, dw):
-        src, dst = c0.at[0, pl.ds(4 + 4 * side, 4)], c0.at[0, pl.ds(12 - 12 * side, 4)]
-        send(from_c + 1 - side, src, dst, dw, 0, 128, sender_x + side)
+        for part in range(2):
+            first = 2 * part if side == 0 else 2 - 2 * part
+            src, dst = c0.at[0, pl.ds(4 + 4 * side + first, 2)], c0.at[0, pl.ds(12 - 12 * side + first, 2)]
+            send(from_c + 1 - side, src, dst, dw, 0, 64, sender_x + side)
 
     @for_sides
     def send_nearest(side, dw):

time: 27.3 us -> 27.3 us (level)
  no operation moved by 1% of the time
where the time goes in v1:
time: 27.3 us; the launch traced here: 27.2 us
  Pallas kernels  26.5 us (97%)
  other arithmetic  0.67 us (2%)
    pallas_call x1, Pallas kernels, per_device(): pl.pallas_call(functools.partial(kernel, wide, narrow), out_shape=[jax.Sh...  26.5 us
    add x1, other arithmetic, per_device(): return kept + added  0.67 us

profile of v1, /device:TPU:65, one launch (start us, length us, event | category | flops | bytes accessed | tf_op | source)
XLA Modules:
  0.0 27.2 jit_solution(11461924553650832931)
XLA Ops:
  0.0 26.5 %shard_map.28 = (f32[8,32,128]{2,1,0:T(8,128)S(1)}, f32[8,32,128]{2,1,0:T(8,128)S(1)}) custom-call(f32[8,32,128]{2,1,0:T(8,128)} %rhs.1, f32[8,32,128]{2,1,0:T(8,128)} %coef.1), custom_call_target="tpu_custom_call" | custom-call | tf_op jit(solution)/shard_map/pallas_call | solution.py:862
  26.5 0.7 %add.3 = f32[8,32,128]{2,1,0:T(8,128)} add(f32[8,32,128]{2,1,0:T(8,128)S(1)} %get-tuple-element.7, f32[8,32,128]{2,1,0:T(8,128)S(1)} %get-tuple-element.8) | non-fusion elementwise | flops 32768 | bytes 393216 | tf_op jit(solution)/shard_map/add | solution.py:872

commit v2 on v1

--- a/solution.py
+++ b/solution.py
@@ -531,8 +531,10 @@
 
     @for_sides
     def send_s_next(side, dw):
-        src = s0.at[0, pl.ds(5 + 4 * side, 2)]
-        send(from_s_next + 1 - side, src, s0.at[0, pl.ds(13 - 12 * side, 2)], dw, 0, 64, sender_x + side)
+        for part in range(2):
+            layer = part if side == 0 else 1 - part
+            src, dst = s0.at[0, 5 + 4 * side + layer], s0.at[0, 13 - 12 * side + layer]
+            send(from_s_next + 1 - side, src, dst, dw, 0, 32, sender_x + side)
 
     steps = cheb(3)
     sweep_a = (level_0.va, level_0.vb, 1, 1, steps[1], True)
@@ -635,7 +637,12 @@
 
     sp[0], sp[1] = squeeze_halves(sk[pl.ds(0, 16), :], sk[pl.ds(16, 16), :])
 
-    for_sides(lambda side, dw: send(from_s1 + 1 - side, sk, k1x.at[1 - side], dw, 0, 32, sender_x + side))
+    @for_sides
+    def send_source(side, dw):
+        for part in range(2):
+            rows = pl.ds(16 * part, 16)
+            send(from_s1 + 1 - side, sk.at[rows], k1x.at[1 - side, rows], dw, 0, 16, sender_x + side)
+
     for_corners(
         lambda side, side_z, dw, dn: send_corner(
             from_s1_corner, sp.at[side_z], k1p.at[1 - side, 1 - side_z], 16, side, side_z

time: 27.3 us -> 27.3 us (level)
  no operation moved by 1% of the time
where the time goes in v2:
time: 27.3 us; the launch traced here: 27.2 us
  Pallas kernels  26.5 us (97%)
  other arithmetic  0.67 us (2%)
    pallas_call x1, Pallas kernels, per_device(): pl.pallas_call(functools.partial(kernel, wide, narrow), out_shape=[jax.Sh...  26.5 us
    add x1, other arithmetic, per_device(): return kept + added  0.67 us

profile of v2, /device:TPU:65, one launch (start us, length us, event | category | flops | bytes accessed | tf_op | source)
XLA Modules:
  0.0 27.2 jit_solution(17087332418525802447)
XLA Ops:
  0.0 26.5 %shard_map.28 = (f32[8,32,128]{2,1,0:T(8,128)S(1)}, f32[8,32,128]{2,1,0:T(8,128)S(1)}) custom-call(f32[8,32,128]{2,1,0:T(8,128)} %rhs.1, f32[8,32,128]{2,1,0:T(8,128)} %coef.1), custom_call_target="tpu_custom_call" | custom-call | tf_op jit(solution)/shard_map/pallas_call | solution.py:869
  26.5 0.7 %add.3 = f32[8,32,128]{2,1,0:T(8,128)} add(f32[8,32,128]{2,1,0:T(8,128)S(1)} %get-tuple-element.7, f32[8,32,128]{2,1,0:T(8,128)S(1)} %get-tuple-element.8) | non-fusion elementwise | flops 32768 | bytes 393216 | tf_op jit(solution)/shard_map/add | solution.py:879
